TPU v7x, 32 devices: a whole 2x2x4 slice. The times are simulated.
32 devices in a mesh: fsdp: 2 (over y), context: 4 (over x, core), tensor: 4 (over z).
Axes of the slice: x: 2, y: 2, z: 4, core: 2. Of those that a mesh axis runs over, the one named last changes fastest.
Arguments:
- inputs: bfloat16 [4096, 1024], P(('fsdp', 'context')), may hold values from -6 to 6
- cotangent: bfloat16 [4096, 1024], P(('fsdp', 'context')), may hold values from -6 to 6
- lengths: int32 [2, 4], P('fsdp'), may hold values from 1 to 2048, as said below
- w_query: float32 [1024, 1024], P(('fsdp', 'context'), 'tensor'), may hold values from -0.1875 to 0.1875
- w_key: float32 [1024, 512], P(('fsdp', 'context'), 'tensor'), may hold values from -0.1875 to 0.1875
- w_value: float32 [1024, 512], P(('fsdp', 'context'), 'tensor'), may hold values from -0.1875 to 0.1875
- w_out: float32 [1024, 1024], P(('fsdp', 'context'), 'tensor'), may hold values from -1.5 to 1.5
- w_gate: float32 [1024, 4608], P(('fsdp', 'context'), 'tensor'), may hold values from -0.1875 to 0.1875
- w_up: float32 [1024, 4608], P(('fsdp', 'context'), 'tensor'), may hold values from -0.1875 to 0.1875
- w_down: float32 [1024, 4608], P(('fsdp', 'context'), 'tensor'), may hold values from -0.09375 to 0.09375
- m_query: float32 [1024, 1024], P(('fsdp', 'context'), 'tensor'), may hold values from -192 to 192
- m_key: float32 [1024, 512], P(('fsdp', 'context'), 'tensor'), may hold values from -192 to 192
- m_value: float32 [1024, 512], P(('fsdp', 'context'), 'tensor'), may hold values from -192 to 192
- m_out: float32 [1024, 1024], P(('fsdp', 'context'), 'tensor'), may hold values from -80 to 80
- m_gate: float32 [1024, 4608], P(('fsdp', 'context'), 'tensor'), may hold values from -112 to 112
- m_up: float32 [1024, 4608], P(('fsdp', 'context'), 'tensor'), may hold values from -112 to 112
- m_down: float32 [1024, 4608], P(('fsdp', 'context'), 'tensor'), may hold values from -224 to 224
- gains: float32 [2176], replicated, may hold values from 0.5 to 1.5
- gain_moment: float32 [2176], replicated, may hold values from -384 to 384
Outputs:
- block_out: bfloat16 [4096, 1024], P(('fsdp', 'context'))
- input_grad: float32 [4096, 1024], P(('fsdp', 'context'))
- mom_query: float32 [1024, 1024], P(('fsdp', 'context'), 'tensor')
- mom_key: float32 [1024, 512], P(('fsdp', 'context'), 'tensor')
- mom_value: float32 [1024, 512], P(('fsdp', 'context'), 'tensor')
- mom_out: float32 [1024, 1024], P(('fsdp', 'context'), 'tensor')
- mom_gate: float32 [1024, 4608], P(('fsdp', 'context'), 'tensor')
- mom_up: float32 [1024, 4608], P(('fsdp', 'context'), 'tensor')
- mom_down: float32 [1024, 4608], P(('fsdp', 'context'), 'tensor')
- new_query: float32 [1024, 1024], P(('fsdp', 'context'), 'tensor')
- new_key: float32 [1024, 512], P(('fsdp', 'context'), 'tensor')
- new_value: float32 [1024, 512], P(('fsdp', 'context'), 'tensor')
- new_out: float32 [1024, 1024], P(('fsdp', 'context'), 'tensor')
- new_gate: float32 [1024, 4608], P(('fsdp', 'context'), 'tensor')
- new_up: float32 [1024, 4608], P(('fsdp', 'context'), 'tensor')
- new_down: float32 [1024, 4608], P(('fsdp', 'context'), 'tensor')
- gain_mom: float32 [2176], replicated
- new_gains: float32 [2176], replicated
Inputs may be any that keep to these rules, and one draw needn't show every extreme that they name: `lengths`: each row sums to 2048; one sequence of each row starts among the first quarter of the stream's tokens and ends in the last quarter.
All inputs are finite; a program needn't handle non-finite values.
Results may differ from a plain program's by a relative error of at most 0.028.
Values may be sent and summed in bfloat16 or wider, within the bound.
A program may use at most 128 MiB of HBM per device.

v0:
```python
import math

import jax
import jax.numpy as jnp
from jax import lax
from jax.sharding import PartitionSpec as P

D = 1024
HEADS = 16
KV_HEADS = 8
HD = 64
NS_STEPS = 5


EPS = 1e-06
THETA = 1000000.0
MU = 0.95
MU_G = 0.9
LR_G = 0.001
NS_A = 3.4445
NS_B = -4.775
NS_C = 2.0315
RATES = (0.1, 0.1, 0.1, 0.8, 0.1, 0.1, 0.1)
FULL_TYPE = jnp.float32
HALF_TYPE = jnp.bfloat16


def rms_scale(values):
    return lax.rsqrt(jnp.mean(values * values, axis=-1, keepdims=True) + EPS)


def rotate(values, cosines, sines_table):
    half_dim = values.shape[-1] // 2
    front_half = values[..., :half_dim]
    back_half = values[..., half_dim:]
    cos_rows = cosines[:, None, :]
    sin_rows = sines_table[:, None, :]
    return jnp.concatenate(
        [
            front_half * cos_rows - back_half * sin_rows,
            back_half * cos_rows + front_half * sin_rows,
        ],
        axis=-1,
    )


def rotate_back(values, cosines, sines_table):
    half_dim = values.shape[-1] // 2
    front_half = values[..., :half_dim]
    back_half = values[..., half_dim:]
    cos_rows = cosines[:, None, :]
    sin_rows = sines_table[:, None, :]
    return jnp.concatenate(
        [
            front_half * cos_rows + back_half * sin_rows,
            back_half * cos_rows - front_half * sin_rows,
        ],
        axis=-1,
    )


def norm_back(upstream, unit_rows, scale_rows, gain_row):
    scaled = upstream * gain_row
    return scale_rows * (scaled - unit_rows * jnp.mean(scaled * unit_rows, axis=-1, keepdims=True))


def stream_layout(row_lengths, points):
    ends = jnp.cumsum(row_lengths)
    after = (points[:, None] >= ends[None, :]).astype(jnp.int32)
    segment = jnp.sum(after, axis=1)
    place = points - jnp.sum(after * row_lengths[None, :], axis=1)
    return (segment, place)


def rope_tables(place):
    freq = THETA ** (-(2.0 * jnp.arange(HD // 2, dtype=FULL_TYPE)) / HD)
    angles = place.astype(FULL_TYPE)[:, None] * freq[None, :]
    return (jnp.cos(angles), jnp.sin(angles))


def newton_schulz(matrix):
    wide = matrix.astype(FULL_TYPE)
    frob_norm = jnp.sqrt(jnp.sum(wide * wide))
    current = (wide / (frob_norm + 1e-07)).astype(HALF_TYPE)
    for repeat in range(NS_STEPS):
        square = lax.dot_general(
            current, current, (((1,), (1,)), ((), ())), preferred_element_type=FULL_TYPE
        ).astype(HALF_TYPE)
        quartic = jnp.dot(square, square, preferred_element_type=FULL_TYPE)
        mixer = (NS_B * square.astype(FULL_TYPE) + NS_C * quartic).astype(HALF_TYPE)
        current = (
            NS_A * current.astype(FULL_TYPE)
            + jnp.dot(mixer, current, preferred_element_type=FULL_TYPE)
        ).astype(HALF_TYPE)
    return current


def gram_newton_schulz(gram_half):
    gram = gram_half.astype(FULL_TYPE)
    size = gram.shape[0]
    diagonal = jnp.arange(size)[:, None] == jnp.arange(size)[None, :]
    norm = jnp.sqrt(jnp.sum(jnp.where(diagonal, gram, 0.0))) + 1e-07
    inverse = 1.0 / norm
    gram = gram * inverse * inverse
    total = None
    for repeat in range(NS_STEPS):
        half = gram.astype(HALF_TYPE)
        mixer_full = NS_B * gram + NS_C * jnp.dot(half, half, preferred_element_type=FULL_TYPE)
        mixer = mixer_full.astype(HALF_TYPE)
        if total is None:
            total = jnp.where(diagonal, NS_A, 0.0) + mixer_full
        else:
            total = NS_A * total + jnp.dot(
                mixer, total.astype(HALF_TYPE), preferred_element_type=FULL_TYPE
            )
        if repeat < NS_STEPS - 1:
            once = NS_A * gram + jnp.dot(mixer, half, preferred_element_type=FULL_TYPE)
            gram = NS_A * once + jnp.dot(
                once.astype(HALF_TYPE), mixer, preferred_element_type=FULL_TYPE
            )
    return (total * inverse).astype(HALF_TYPE)


def head_rows(values, head_index, group_size):
    picked = values[:, head_index * group_size : (head_index + 1) * group_size, :]
    return picked.transpose(1, 0, 2).reshape(group_size * values.shape[0], values.shape[2])


def body(
    inputs,
    cotangent,
    lengths,
    w_query,
    w_key,
    w_value,
    w_out,
    w_gate,
    w_up,
    w_down,
    m_query,
    m_key,
    m_value,
    m_out,
    m_gate,
    m_up,
    m_down,
    gains,
    gain_moment,
):
    masters = (w_query, w_key, w_value, w_out, w_gate, w_up, w_down)
    moments = (m_query, m_key, m_value, m_out, m_gate, m_up, m_down)
    rows_here = inputs.shape[0]
    context_size = lax.axis_size("context")
    tensor_size = lax.axis_size("tensor")
    span = context_size * rows_here
    offset = lax.axis_index("context") * rows_here
    local_q = w_query.shape[1] // HD
    local_kv = w_key.shape[1] // HD
    group_size = HEADS // KV_HEADS
    scale = HD ** (-0.5)
    gain_one = gains[:D]
    gain_two = gains[D : 2 * D]
    gain_query = gains[2 * D : 2 * D + HD]
    gain_key = gains[2 * D + HD :]
    points = jnp.arange(span, dtype=jnp.int32)
    segment, place = stream_layout(lengths[0], points)
    query_points = offset + jnp.arange(rows_here, dtype=jnp.int32)
    query_segment = lax.dynamic_slice_in_dim(segment, offset, rows_here)
    query_place = lax.dynamic_slice_in_dim(place, offset, rows_here)
    allowed = (query_segment[:, None] == segment[None, :]) & (
        points[None, :] <= query_points[:, None]
    )
    allowed_rows = jnp.concatenate([allowed] * group_size, axis=0)
    cosines, sines_table = rope_tables(query_place)
    half_q = w_query.astype(HALF_TYPE)
    half_k = w_key.astype(HALF_TYPE)
    half_v = w_value.astype(HALF_TYPE)
    half_o = w_out.astype(HALF_TYPE)
    half_g = w_gate.astype(HALF_TYPE)
    half_u = w_up.astype(HALF_TYPE)
    half_d = w_down.astype(HALF_TYPE)
    plane = ("fsdp", "context")
    width_q, width_k, width_f = w_query.shape[1], w_key.shape[1], w_gate.shape[1]
    full_qkv = lax.all_gather(
        jnp.concatenate([half_q, half_k, half_v], axis=1), plane, axis=0, tiled=True
    )
    full_o = lax.all_gather(half_o, plane, axis=0, tiled=True)
    full_gu = lax.all_gather(
        jnp.concatenate([half_g, half_u], axis=1), plane, axis=0, tiled=True
    )
    full_d = lax.all_gather(half_d, plane, axis=0, tiled=True)
    rows = inputs.astype(FULL_TYPE)
    scale_one = rms_scale(rows)
    unit_one = rows * scale_one
    normed = (unit_one * gain_one).astype(HALF_TYPE)
    qkv_raw = jnp.dot(normed, full_qkv, preferred_element_type=FULL_TYPE)
    query_raw = qkv_raw[:, :width_q].reshape(rows_here, local_q, HD)
    key_raw = qkv_raw[:, width_q : width_q + width_k].reshape(rows_here, local_kv, HD)
    value_half = qkv_raw[:, width_q + width_k :].astype(HALF_TYPE)
    scale_q = rms_scale(query_raw)
    unit_q = query_raw * scale_q
    query_half = rotate(unit_q * gain_query, cosines, sines_table).astype(HALF_TYPE)
    scale_k = rms_scale(key_raw)
    unit_k = key_raw * scale_k
    key_half = rotate(unit_k * gain_key, cosines, sines_table).astype(HALF_TYPE)
    key_value = lax.all_gather(
        jnp.concatenate([key_half.reshape(rows_here, local_kv * HD), value_half], axis=1),
        "context",
        axis=0,
        tiled=True,
    )
    key_all = key_value[:, :width_k]
    value_all = key_value[:, width_k:]

    def head_scores(query_rows, key_cols):
        scores = (
            jnp.einsum("qd,kd->qk", query_rows, key_cols, preferred_element_type=FULL_TYPE) * scale
        )
        return jnp.where(allowed_rows, scores, -1e30)

    mixed_parts = []
    lse_parts = []
    for head_index in range(local_kv):
        query_rows = head_rows(query_half, head_index, group_size)
        key_cols = key_all[:, head_index * HD : (head_index + 1) * HD]
        value_cols = value_all[:, head_index * HD : (head_index + 1) * HD]
        scores = head_scores(query_rows, key_cols)
        peak = jnp.max(scores, axis=-1, keepdims=True)
        expo = jnp.exp(scores - peak)
        denom = jnp.sum(expo, axis=-1, keepdims=True)
        probs = (expo / denom).astype(HALF_TYPE)
        lse_parts.append(peak + jnp.log(denom))
        head_out = jnp.dot(probs, value_cols, preferred_element_type=FULL_TYPE).astype(HALF_TYPE)
        mixed_parts.append(head_out.reshape(group_size, rows_here, HD).transpose(1, 0, 2))
    mixed = jnp.concatenate(mixed_parts, axis=1).reshape(rows_here, local_q * HD)
    attn_part = jnp.einsum("tc,dc->td", mixed, full_o, preferred_element_type=FULL_TYPE)
    attended = lax.psum(attn_part.astype(jnp.bfloat16), "tensor").astype(jnp.float32)
    resid = rows + attended
    scale_two = rms_scale(resid)
    unit_two = resid * scale_two
    second = (unit_two * gain_two).astype(HALF_TYPE)
    gate_up = jnp.dot(second, full_gu, preferred_element_type=FULL_TYPE)
    gate = gate_up[:, :width_f]
    up_proj = gate_up[:, width_f:]
    sigmoid_gate = jax.nn.sigmoid(gate)
    swish = gate * sigmoid_gate
    hidden = (swish * up_proj).astype(HALF_TYPE)
    ffn_part = jnp.einsum("tf,df->td", hidden, full_d, preferred_element_type=FULL_TYPE)
    d_hidden = jnp.dot(cotangent, full_d, preferred_element_type=FULL_TYPE)
    grad_down = jnp.einsum("td,tf->df", cotangent, hidden, preferred_element_type=FULL_TYPE)
    d_gate = (d_hidden * up_proj * sigmoid_gate * (1.0 + gate * (1.0 - sigmoid_gate))).astype(
        HALF_TYPE
    )
    d_up = (d_hidden * swish).astype(HALF_TYPE)
    d_gate_up = jnp.concatenate([d_gate, d_up], axis=1)
    grad_gate_up = jnp.einsum("td,tf->df", second, d_gate_up, preferred_element_type=FULL_TYPE)
    wide_grad = lax.psum_scatter(
        jnp.concatenate(
            [grad_gate_up.astype(jnp.bfloat16), grad_down.astype(jnp.bfloat16)], axis=1
        ),
        plane,
        scatter_dimension=0,
        tiled=True,
    ).astype(jnp.float32)
    d_second_part = jnp.einsum(
        "tf,df->td", d_gate_up, full_gu, preferred_element_type=FULL_TYPE
    )
    d_second = lax.psum(d_second_part.astype(jnp.bfloat16), "tensor").astype(jnp.float32)
    ffn_half, d_second = lax.optimization_barrier((ffn_part.astype(jnp.bfloat16), d_second))
    ffn_out = lax.psum(ffn_half, "tensor").astype(jnp.float32)
    block_out = (resid + ffn_out).astype(HALF_TYPE)
    d_resid = cotangent.astype(FULL_TYPE) + norm_back(d_second, unit_two, scale_two, gain_two)
    grad_gain_two = jnp.sum(d_second * unit_two, axis=0)
    d_attn = d_resid.astype(HALF_TYPE)
    grad_out = jnp.einsum("td,tc->dc", d_attn, mixed, preferred_element_type=FULL_TYPE)
    d_mixed = (
        jnp.dot(d_attn, full_o, preferred_element_type=FULL_TYPE)
        .astype(HALF_TYPE)
        .reshape(rows_here, local_q, HD)
    )
    d_query_parts = []
    d_key_parts = []
    d_value_parts = []
    for head_index in range(local_kv):
        query_rows = head_rows(query_half, head_index, group_size)
        grad_rows = head_rows(d_mixed, head_index, group_size)
        key_cols = key_all[:, head_index * HD : (head_index + 1) * HD]
        value_cols = value_all[:, head_index * HD : (head_index + 1) * HD]
        scores = head_scores(query_rows, key_cols)
        probs_full = jnp.exp(scores - lse_parts[head_index])
        probs_half = probs_full.astype(HALF_TYPE)
        d_probs = jnp.einsum("qd,kd->qk", grad_rows, value_cols, preferred_element_type=FULL_TYPE)
        delta = jnp.sum(probs_full * d_probs, axis=-1, keepdims=True)
        d_scores = (probs_full * (d_probs - delta)).astype(HALF_TYPE)
        d_query_rows = jnp.dot(d_scores, key_cols, preferred_element_type=FULL_TYPE) * scale
        d_query_parts.append(d_query_rows.reshape(group_size, rows_here, HD).transpose(1, 0, 2))
        d_key_parts.append(
            jnp.einsum("qk,qd->kd", d_scores, query_rows, preferred_element_type=FULL_TYPE) * scale
        )
        d_value_parts.append(
            jnp.einsum("qk,qd->kd", probs_half, grad_rows, preferred_element_type=FULL_TYPE)
        )
    d_key_all = jnp.concatenate(d_key_parts, axis=1)
    d_value_all = jnp.concatenate(d_value_parts, axis=1)
    key_value_grad = lax.psum_scatter(
        jnp.concatenate([d_key_all, d_value_all], axis=1).astype(jnp.bfloat16),
        "context",
        scatter_dimension=0,
        tiled=True,
    ).astype(jnp.float32)
    key_grad = key_value_grad[:, :width_k]
    value_grad = key_value_grad[:, width_k:]
    d_value_raw = value_grad.astype(HALF_TYPE)
    d_key_normed = rotate_back(key_grad.reshape(rows_here, local_kv, HD), cosines, sines_table)
    grad_gain_key = jnp.sum(d_key_normed * unit_k, axis=(0, 1))
    d_key_raw = (
        norm_back(d_key_normed, unit_k, scale_k, gain_key)
        .astype(HALF_TYPE)
        .reshape(rows_here, local_kv * HD)
    )
    d_query_normed = rotate_back(jnp.concatenate(d_query_parts, axis=1), cosines, sines_table)
    grad_gain_query = jnp.sum(d_query_normed * unit_q, axis=(0, 1))
    d_query_raw = (
        norm_back(d_query_normed, unit_q, scale_q, gain_query)
        .astype(HALF_TYPE)
        .reshape(rows_here, local_q * HD)
    )
    d_qkv = jnp.concatenate([d_query_raw, d_key_raw, d_value_raw], axis=1)
    grad_qkv = jnp.einsum("td,tc->dc", normed, d_qkv, preferred_element_type=FULL_TYPE)
    narrow_grad = lax.psum_scatter(
        jnp.concatenate([grad_qkv.astype(jnp.bfloat16), grad_out.astype(jnp.bfloat16)], axis=1),
        plane,
        scatter_dimension=0,
        tiled=True,
    ).astype(jnp.float32)
    d_normed_part = jnp.einsum("tc,dc->td", d_qkv, full_qkv, preferred_element_type=FULL_TYPE)
    d_normed_half, block_out = lax.optimization_barrier(
        (d_normed_part.astype(jnp.bfloat16), block_out)
    )
    d_normed = lax.psum(d_normed_half, "tensor").astype(jnp.float32)
    input_grad = d_resid + norm_back(d_normed, unit_one, scale_one, gain_one)
    grad_gain_one = jnp.sum(d_normed * unit_one, axis=0)
    first_tensor = (lax.axis_index("tensor") == 0).astype(FULL_TYPE)
    gain_local = jnp.concatenate(
        [grad_gain_one * first_tensor, grad_gain_two * first_tensor, grad_gain_query, grad_gain_key]
    )
    gain_total = lax.psum(gain_local, ("fsdp", "context", "tensor"))
    reduced = (
        narrow_grad[:, :width_q],
        narrow_grad[:, width_q : width_q + width_k],
        narrow_grad[:, width_q + width_k : width_q + 2 * width_k],
        narrow_grad[:, width_q + 2 * width_k :],
        wide_grad[:, :width_f],
        wide_grad[:, width_f : 2 * width_f],
        wide_grad[:, 2 * width_f :],
    )
    new_moments = tuple(
        (MU * moment_old + gradient for moment_old, gradient in zip(moments, reduced))
    )
    row_block = w_gate.shape[0]
    plane_size = lax.axis_size("fsdp") * context_size
    plane_index = lax.axis_index("fsdp") * context_size + lax.axis_index("context")
    wide_all = lax.all_gather(
        jnp.concatenate([moment.astype(HALF_TYPE) for moment in new_moments[4:]], axis=1),
        plane,
        axis=0,
        tiled=True,
    )
    wide_rows = lax.dynamic_slice_in_dim(wide_all, plane_index * row_block, row_block)
    wide = [wide_all[:, index * width_f : (index + 1) * width_f] for index in range(3)]
    gram_rows = jnp.stack(
        [
            lax.dot_general(
                wide_rows[:, index * width_f : (index + 1) * width_f],
                wide[index],
                (((1,), (1,)), ((), ())),
                preferred_element_type=FULL_TYPE,
            )
            for index in range(3)
        ]
    )
    gram_rows = lax.psum(gram_rows, "tensor").astype(HALF_TYPE)
    gram = lax.all_to_all(
        jnp.concatenate(
            [gram_rows, jnp.zeros((plane_size - 3, row_block, D), HALF_TYPE)], axis=0
        ),
        plane,
        split_axis=0,
        concat_axis=0,
        tiled=True,
    ).reshape(D, D)
    narrow = jnp.stack(
        [
            jnp.pad(moment.astype(HALF_TYPE), ((0, 0), (0, width_q - moment.shape[1])))
            for moment in new_moments[:4]
        ]
    )
    narrow_rows = (
        lax.all_to_all(narrow, "tensor", split_axis=0, concat_axis=0, tiled=True)
        .transpose(1, 0, 2)
        .reshape(row_block, tensor_size * width_q)
    )
    narrow_all = lax.all_gather(narrow_rows, plane, axis=0, tiled=True)
    ready = lax.cond(
        plane_index < 3,
        lambda gram_arg, narrow_arg: gram_newton_schulz(gram_arg),
        lambda gram_arg, narrow_arg: newton_schulz(narrow_arg),
        gram,
        narrow_all,
    )
    back_rows = lax.all_to_all(
        ready.reshape(plane_size, row_block, D), plane, split_axis=0, concat_axis=0, tiled=True
    )
    narrow_back = lax.all_to_all(
        back_rows[3].reshape(row_block, tensor_size, width_q).transpose(1, 0, 2),
        "tensor",
        split_axis=0,
        concat_axis=0,
        tiled=True,
    )
    ortho = [narrow_back[index, :, : masters[index].shape[1]] for index in range(4)] + [
        jnp.dot(back_rows[index], wide[index], preferred_element_type=FULL_TYPE).astype(HALF_TYPE)
        for index in range(3)
    ]
    new_weights = []
    for index in range(len(RATES)):
        columns = masters[index].shape[1]
        rate = RATES[index] * 0.2 * math.sqrt(max(D, columns * tensor_size))
        new_weights.append(masters[index] - rate * ortho[index].astype(FULL_TYPE))
    gain_mom = MU_G * gain_moment + gain_total
    new_gains = gains - LR_G * gain_mom
    return (
        block_out,
        input_grad,
        new_moments[0],
        new_moments[1],
        new_moments[2],
        new_moments[3],
        new_moments[4],
        new_moments[5],
        new_moments[6],
        new_weights[0],
        new_weights[1],
        new_weights[2],
        new_weights[3],
        new_weights[4],
        new_weights[5],
        new_weights[6],
        gain_mom,
        new_gains,
    )


def solution(mesh):
    in_specs = (
        P(("fsdp", "context"), None),
        P(("fsdp", "context"), None),
        P("fsdp", None),
        P(("fsdp", "context"), "tensor"),
        P(("fsdp", "context"), "tensor"),
        P(("fsdp", "context"), "tensor"),
        P(("fsdp", "context"), "tensor"),
        P(("fsdp", "context"), "tensor"),
        P(("fsdp", "context"), "tensor"),
        P(("fsdp", "context"), "tensor"),
        P(("fsdp", "context"), "tensor"),
        P(("fsdp", "context"), "tensor"),
        P(("fsdp", "context"), "tensor"),
        P(("fsdp", "context"), "tensor"),
        P(("fsdp", "context"), "tensor"),
        P(("fsdp", "context"), "tensor"),
        P(("fsdp", "context"), "tensor"),
        P(),
        P(),
    )
    out_specs = (
        P(("fsdp", "context"), None),
        P(("fsdp", "context"), None),
        P(("fsdp", "context"), "tensor"),
        P(("fsdp", "context"), "tensor"),
        P(("fsdp", "context"), "tensor"),
        P(("fsdp", "context"), "tensor"),
        P(("fsdp", "context"), "tensor"),
        P(("fsdp", "context"), "tensor"),
        P(("fsdp", "context"), "tensor"),
        P(("fsdp", "context"), "tensor"),
        P(("fsdp", "context"), "tensor"),
        P(("fsdp", "context"), "tensor"),
        P(("fsdp", "context"), "tensor"),
        P(("fsdp", "context"), "tensor"),
        P(("fsdp", "context"), "tensor"),
        P(("fsdp", "context"), "tensor"),
        P(),
        P(),
    )
    return jax.shard_map(body, mesh=mesh, in_specs=in_specs, out_specs=out_specs, check_vma=False)
```

profile of v0, /device:TPU:0, one launch (start us, length us, event | category | flops | bytes accessed | tf_op | source)
XLA Modules:
  0.0 823.4 jit_solution(5165547167072875428)
XLA Ops:
  15.7 21.2 %all-gather.7.cloned.1.call-done = bf16[1024,512]{1,0:T(8,128)(2,1)} async-done(((bf16[128,512]{1,0:T(8,128)(2,1)}), bf16[1024,512]{1,0:T(8,128)(2,1)}) %all-gather.7.cloned.1.call-update) | async-done | bytes 1048592 | tf_op jit(solution)/shard_map/all_gather | solution.py:184
  36.9 2.4 fusion.164
  40.6 9.8 %all_gather.26 = bf16[1024,256]{1,0:T(8,128)(2,1)S(1)} all-gather(bf16[128,256]{1,0:T(8,128)(2,1)S(1)} %convert_element_type.373), channel_id=1, replica_groups=mesh['fsdp'=2,'context'=4,'tensor'=4] {'fsdp','context'}, dimensions={0}, use_global_device_ids=true | all-gather | bytes 589824 | tf_op jit(solution)/shard_map/all_gather | solution.py:187
  53.0 4.3 all-gather.9.cloned.1.call-done
  57.2 2.9 fusion.200
  75.5 48.5 %all-reduce.9.cloned.1.call-done = bf16[512,1024]{1,0:T(8,128)(2,1)} async-done(((bf16[512,1024]{1,0:T(8,128)(2,1)}), bf16[512,1024]{1,0:T(8,128)(2,1)}) %all-reduce.9.cloned.1.call-update) | async-done | bytes 1048592 | tf_op jit(solution)/shard_map/psum | solution.py:237
  125.6 39.1 %all-gather.11.cloned.1.call-done = bf16[1024,2304]{1,0:T(8,128)(2,1)} async-done(((bf16[128,2304]{1,0:T(8,128)(2,1)}), bf16[1024,2304]{1,0:T(8,128)(2,1)}) %all-gather.11.cloned.1.call-update) | async-done | bytes 4718608 | tf_op jit(solution)/shard_map/all_gather | solution.py:188
  164.8 7.7 fusion.190
  172.5 23.8 %all-gather.13.cloned.1.call-done = bf16[1024,1152]{1,0:T(8,128)(2,1)} async-done(((bf16[128,1152]{1,0:T(8,128)(2,1)}), bf16[1024,1152]{1,0:T(8,128)(2,1)}) %all-gather.13.cloned.1.call-update) | async-done | bytes 2359312 | tf_op jit(solution)/shard_map/all_gather | solution.py:191
  196.3 6.4 multiply_convert_fusion.3
  204.1 3.6 fusion.145
  207.8 4.2 convolution_convert_fusion.5
  212.0 47.7 %all-reduce.11.cloned.1.call-done = bf16[512,1024]{1,0:T(8,128)(2,1)} async-done(((bf16[512,1024]{1,0:T(8,128)(2,1)}), bf16[512,1024]{1,0:T(8,128)(2,1)}) %all-reduce.11.cloned.1.call-update) | async-done | bytes 1048592 | tf_op jit(solution)/shard_map/psum | solution.py:268
  263.5 2.6 multiply_reduce_fusion.2
  266.6 47.3 %all-reduce.13.cloned.1.call-done = bf16[512,1024]{1,0:T(8,128)(2,1)} async-done(((bf16[512,1024]{1,0:T(8,128)(2,1)}), bf16[512,1024]{1,0:T(8,128)(2,1)}) %all-reduce.13.cloned.1.call-update) | async-done | bytes 1048592 | tf_op jit(solution)/shard_map/psum | solution.py:270
  313.9 4.5 add_convert_fusion.13
  319.3 5.8 fusion.125
  325.1 4.4 multiply_reduce_fusion
  329.6 4.6 multiply_convert_fusion
  336.6 4.4 multiply_reduce_fusion.1
  341.0 4.5 multiply_convert_fusion.1
  349.8 4.8 fusion.104
  354.5 5.0 convolution_convert_fusion
  359.5 6.3 pad_maximum_fusion
  370.4 4.3 convolution_multiply_fusion.2
  376.6 4.3 convolution_multiply_fusion.3
  396.6 46.3 %reduce-scatter.8.cloned.1.call-done = bf16[128,3456]{1,0:T(8,128)(2,1)} async-done(((bf16[1024,3456]{1,0:T(8,128)(2,1)}), bf16[128,3456]{1,0:T(8,128)(2,1)}) %reduce-scatter.8.cloned.1.call-update) | async-done | bytes 884752 | tf_op jit(solution)/shard_map/reduce_scatter | solution.py:257
  447.1 37.8 %reduce-scatter.10.cloned.1.call-done = bf16[128,768]{1,0:T(8,128)(2,1)} async-done(((bf16[1024,768]{1,0:T(8,128)(2,1)}), bf16[128,768]{1,0:T(8,128)(2,1)}) %reduce-scatter.10.cloned.1.call-update) | async-done | bytes 196624
  488.2 4.6 all-to-all-start
  493.2 8.5 %all-to-all-done = bf16[4,128,256]{1,2,0:T(8,128)(2,1)S(1)} async-done(((bf16[4,128,256]{1,2,0:T(8,128)(2,1)}), bf16[4,128,256]{1,2,0:T(8,128)(2,1)S(1)}, u32[]{:S(2)}, u32[]{:S(2)}) %all-to-all-start) | async-done | bytes 262176 | tf_op jit(solution)/shard_map/all_to_all | solution.py:399
  502.6 33.2 %all-gather.17.cloned.1.call-done = bf16[1024,3456]{1,0:T(8,128)(2,1)} async-done(((bf16[128,3456]{1,0:T(8,128)(2,1)}), bf16[1024,3456]{1,0:T(8,128)(2,1)}) %all-gather.17.cloned.1.call-update) | async-done | bytes 7077904 | tf_op jit(solution)/shard_map/all_gather | solution.py:363
  535.8 2.6 fusion.146
  538.5 2.7 fusion.152
  541.1 2.7 fusion.149
  544.0 61.1 %all-reduce.16 = bf16[3,128,1024]{2,1,0:T(8,128)(2,1)S(1)} all-reduce(f32[3,128,1024]{2,1,0:T(8,128)S(1)} %pad_maximum_fusion.3), channel_id=1, replica_groups=mesh['fsdp'=2,'context'=4,'tensor'=4] {'tensor'}, use_global_device_ids=true, to_apply=%region_24.25 | all-reduce | flops 393216 | bytes 2359296 | tf_op jit(solution)/shard_map/psum | solution.py:382
  606.8 3.6 all-to-all-start.1
  610.5 3.0 convolution_convert_fusion.8
  613.5 23.4 %all-to-all-done.1 = bf16[8,128,1024]{2,1,0:T(8,128)(2,1)S(1)} async-done(((bf16[8,128,1024]{2,1,0:T(8,128)(2,1)}), bf16[8,128,1024]{2,1,0:T(8,128)(2,1)S(1)}, u32[]{:S(2)}, u32[]{:S(2)}) %all-to-all-start.1) | async-done | bytes 2097184 | tf_op jit(solution)/shard_map/all_to_all | solution.py:383
  637.0 76.0 %conditional.3 = (bf16[1024,1024]{1,0:T(8,128)(2,1)}) conditional(s32[]{:T(128)} %convert_element_type.405, bf16[1024,1024]{1,0:T(8,128)(2,1)} %all-gather.15.cloned.1.call-done, bf16[8,128,1024]{2,1,0:T(8,128)(2,1)S(1)} %all-to-all-done.1), branch_computations={%region_25.27_spmd, %region_27.29_spmd} | conditional | flops 36595302400 | bytes 226500704
  645.6 2.6 fusion.30
  650.2 2.4 bitcast_add_fusion.1
  652.6 2.4 bitcast_add_fusion
  654.9 2.4 multiply_add_fusion.9
  657.3 2.5 add_convert_fusion.12
  659.8 2.3 fusion.76
  662.2 3.2 multiply_add_fusion.6
  665.4 2.5 add_convert_fusion.11
  667.9 2.4 fusion.73
  670.3 2.7 multiply_add_fusion.3
  673.0 2.5 add_convert_fusion.10
  675.5 2.4 multiply_add_fusion.10
  677.9 2.4 multiply_add_fusion.8
  680.3 4.6 fusion.47
  684.8 2.4 multiply_add_fusion.2
  689.1 4.3 fusion.45
  693.5 19.3 %add_multiply_fusion = bf16[1024,1024]{1,0:T(8,128)(2,1)} fusion(f32[]{:T(128)S(6)} %div.16, f32[1024,1024]{1,0:T(8,128)} %fusion.47, f32[1024,1024]{1,0:T(8,128)} %copy-done.70, f32[1024,1024]{1,0:T(8,128)} %fusion.45, f32[1024,1024]{1,0:T(8,128)} %copy-done.71), kind=kOutput, calls=%fused_computation.39 | convolution fusion | flops 4313841664 | bytes 18874372 | tf_op jit(solution)/shard_map/cond/branch_1_fun/dot_general | solution.py:113
  713.0 18.5 %all-to-all-start.2 = ((bf16[8,128,1024]{2,1,0:T(8,128)(2,1)}), bf16[8,128,1024]{2,1,0:T(8,128)(2,1)}, u32[]{:S(2)}, u32[]{:S(2)}) async-start(bf16[8,128,1024]{2,1,0:T(8,128)(2,1)} %bitcast.37), calls=%async_computation.4 | async-start | bytes 4194304 | tf_op jit(solution)/shard_map/all_to_all | solution.py:411
  737.8 2.0 fusion.132
  739.9 49.6 %psum.47 = f32[2176]{0:T(1024)S(1)} all-reduce(f32[2176]{0:T(1024)S(1)} %concatenate.80), channel_id=1, replica_groups=mesh['fsdp'=2,'context'=4,'tensor'=4] {'fsdp','context','tensor'}, use_global_device_ids=true, to_apply=%region_35.36 | all-reduce | flops 2176 | bytes 17408 | tf_op jit(solution)/shard_map/psum | solution.py:347
  790.9 3.2 fusion.129
  800.5 3.5 all-to-all-start.3
  804.0 3.3 fusion.118
  807.3 3.1 fusion.115
  810.5 3.1 fusion.112
  (318 shorter events, 94.8 us)
Async XLA Ops:
  7.2 29.7 %all-gather.7.cloned.1.call-start = ((), (), s32[]{:S(2)}) async-start(), calls=%async_computation.7 | async-start | bytes 1179648 | tf_op jit(solution)/shard_map/all_gather | solution.py:184
  10.5 46.7 %all-gather.9.cloned.1.call-start = ((), (), s32[]{:S(2)}) async-start(), calls=%async_computation.8 | async-start | bytes 1310720 | tf_op jit(solution)/shard_map/all_gather | solution.py:206
  13.8 25.5 %copy-start.55 = (f32[512]{0:T(512)}, f32[512]{0:T(512)S(1)}, u32[]{:S(2)}) copy-start(f32[512]{0:T(512)S(1)} %add_rsqrt_fusion.3) | copy-start | bytes 6148
  14.6 25.7 %copy-start.66 = (f32[64]{0:T(128)}, f32[64]{0:T(128)S(1)}, u32[]{:S(2)}) copy-start(f32[64]{0:T(128)S(1)} %get-tuple-element.190) | copy-start | bytes 772
  14.6 37.0 %copy-start.64 = (f32[64]{0:T(128)}, f32[64]{0:T(128)S(1)}, u32[]{:S(2)}) copy-start(f32[64]{0:T(128)S(1)} %get-tuple-element.191) | copy-start | bytes 772
  15.4 24.1 %copy-start.50 = (f32[1024]{0:T(1024)}, f32[1024]{0:T(1024)S(1)}, u32[]{:S(2)}) copy-start(f32[1024]{0:T(1024)S(1)} %get-tuple-element.189) | copy-start | bytes 12292
  15.4 149.4 %copy-start.53 = (f32[1024]{0:T(1024)}, f32[1024]{0:T(1024)S(1)}, u32[]{:S(2)}) copy-start(f32[1024]{0:T(1024)S(1)} %get-tuple-element.188) | copy-start | bytes 12292
  39.3 12.8 %copy-start.10 = (f32[512,512]{0,1:T(8,128)}, f32[512,512]{0,1:T(8,128)S(1)}, u32[]{:S(2)}) copy-start(f32[512,512]{0,1:T(8,128)S(1)} %fusion.164) | copy-start | bytes 3145732
  40.4 83.6 %all-reduce.9.cloned.1.call-start = ((), (), s32[]{:S(2)}) async-start(), calls=%async_computation.9 | async-start | bytes 2097152 | tf_op jit(solution)/shard_map/psum | solution.py:237
  50.3 20.2 %copy-start.12 = (bf16[1024,256]{1,0:T(8,128)(2,1)}, bf16[1024,256]{1,0:T(8,128)(2,1)S(1)}, u32[]{:S(2)}) copy-start(bf16[1024,256]{1,0:T(8,128)(2,1)S(1)} %all_gather.26) | copy-start | bytes 1572868
  51.5 8.7 %copy-start.19 = (pred[512,2048]{1,0:T(32,128)(4,1)}, pred[512,2048]{1,0:T(32,128)(4,1)S(1)}, u32[]{:S(2)}) copy-start(pred[512,2048]{1,0:T(32,128)(4,1)S(1)} %fusion.101) | copy-start | bytes 3145732
  52.9 7.3 copy-start.33
  53.0 8.6 %copy-start.31 = (bf16[8,8,2,512]{3,1,2,0:T(8,128)(2,1)}, bf16[8,8,2,512]{3,1,2,0:T(8,128)(2,1)S(1)}, u32[]{:S(2)}) copy-start(bf16[8,8,2,512]{3,1,2,0:T(8,128)(2,1)S(1)} %copy.160) | copy-start | bytes 393220
  60.2 6.3 copy-start.1
  60.2 6.3 copy-start.59
  61.5 5.0 copy-start.61
  72.0 52.0 %copy-start.4 = (bf16[512,1024]{1,0:T(8,128)(2,1)S(1)}, bf16[512,1024]{1,0:T(8,128)(2,1)}, u32[]{:S(2)}) copy-start(bf16[512,1024]{1,0:T(8,128)(2,1)} %param.21) | copy-start | bytes 3145732
  72.0 92.8 %all-gather.11.cloned.1.call-start = ((), (), s32[]{:S(2)}) async-start(), calls=%async_computation.10 | async-start | bytes 5308416 | tf_op jit(solution)/shard_map/all_gather | solution.py:188
  73.0 123.3 %all-gather.13.cloned.1.call-start = ((), (), s32[]{:S(2)}) async-start(), calls=%async_computation.11 | async-start | bytes 2654208 | tf_op jit(solution)/shard_map/all_gather | solution.py:191
  74.9 184.8 %all-reduce.11.cloned.1.call-start = ((), (), s32[]{:S(2)}) async-start(), calls=%async_computation.12 | async-start | bytes 2097152 | tf_op jit(solution)/shard_map/psum | solution.py:268
  125.6 46.8 %copy-start.57 = (f32[512]{0:T(512)}, f32[512]{0:T(512)S(1)}, u32[]{:S(2)}) copy-start(f32[512]{0:T(512)S(1)} %add_rsqrt_fusion.2) | copy-start | bytes 6148
  164.8 31.5 %copy-start.21 = (bf16[512,1024]{1,0:T(8,128)(2,1)S(1)}, bf16[512,1024]{1,0:T(8,128)(2,1)}, u32[]{:S(2)}) copy-start(bf16[512,1024]{1,0:T(8,128)(2,1)} %param.22) | copy-start | bytes 3145732
  196.3 7.8 copy-start.69
  207.7 106.1 %all-reduce.13.cloned.1.call-start = ((), (), s32[]{:S(2)}) async-start(), calls=%async_computation.14 | async-start | bytes 2097152 | tf_op jit(solution)/shard_map/psum | solution.py:270
  212.0 49.4 %copy-start.60 = (f32[1024]{0:T(1024)S(1)}, f32[1024]{0:T(1024)}, u32[]{:S(2)}) copy-start(f32[1024]{0:T(1024)} %copy-done.59) | copy-start | bytes 12292
  261.2 5.4 copy-start.8
  261.2 127.8 %reduce-scatter.6.cloned.1.call-start = ((), (), s32[]{:S(2)}) async-start(), calls=%async_computation.13 | async-start | bytes 1310720 | tf_op jit(solution)/shard_map/reduce_scatter | solution.py:305
  313.9 11.2 %slice-start.2 = ((s8[8388608]{0:T(1024)(128)(4,1)}), s8[4194304]{0:T(1024)(128)(4,1)S(1)}, s32[]{:S(2)}) async-start(s8[8388608]{0:T(1024)(128)(4,1)} %bitcast.202), calls=%async_computation.22 | async-start | bytes 8388608
  318.4 69.4 %copy-start.6 = (f32[512,1024]{1,0:T(8,128)}, f32[512,1024]{1,0:T(8,128)S(1)}, u32[]{:S(2)}) copy-start(f32[512,1024]{1,0:T(8,128)S(1)} %get-tuple-element.153) | copy-start | bytes 6291460
  318.4 6.7 slice-start.3
  319.3 5.8 copy-start.18
  325.1 9.9 %slice-start = ((s8[8388608]{0:T(1024)(128)(4,1)}), s8[4194304]{0:T(1024)(128)(4,1)S(1)}, s32[]{:S(2)}) async-start(s8[8388608]{0:T(1024)(128)(4,1)} %bitcast.200), calls=%async_computation.20 | async-start | bytes 8388608
  329.6 5.5 slice-start.1
  341.0 6.5 copy-start.32
  349.4 5.1 copy-start.54
  349.5 93.5 %reduce-scatter.8.cloned.1.call-start = ((), (), s32[]{:S(2)}) async-start(), calls=%async_computation.16 | async-start | bytes 7962624 | tf_op jit(solution)/shard_map/reduce_scatter | solution.py:257
  349.7 4.8 copy-start.9
  349.7 4.8 copy-start.58
  349.7 4.8 copy-start.74
  365.9 119.0 %reduce-scatter.10.cloned.1.call-start = ((), (), s32[]{:S(2)}) async-start(), calls=%async_computation.19 | async-start | bytes 1769472
  387.8 5.2 copy-start.51
  387.8 5.2 copy-start.56
  394.9 49.3 %copy-start.22 = (f32[128,1152]{1,0:T(8,128)S(1)}, f32[128,1152]{1,0:T(8,128)}, u32[]{:S(2)}) copy-start(f32[128,1152]{1,0:T(8,128)} %param.37) | copy-start | bytes 1769476
  394.9 49.3 %copy-start.23 = (f32[128,1152]{1,0:T(8,128)S(1)}, f32[128,1152]{1,0:T(8,128)}, u32[]{:S(2)}) copy-start(f32[128,1152]{1,0:T(8,128)} %param.36) | copy-start | bytes 1769476
  394.9 49.3 %copy-start.24 = (f32[128,1152]{1,0:T(8,128)S(1)}, f32[128,1152]{1,0:T(8,128)}, u32[]{:S(2)}) copy-start(f32[128,1152]{1,0:T(8,128)} %param.35) | copy-start | bytes 1769476
  396.6 139.2 %all-gather.17.cloned.1.call-start = ((), (), s32[]{:S(2)}) async-start(), calls=%async_computation.18 | async-start | bytes 7962624 | tf_op jit(solution)/shard_map/all_gather | solution.py:363
  488.2 13.5 %all-to-all-start = ((bf16[4,128,256]{1,2,0:T(8,128)(2,1)}), bf16[4,128,256]{1,2,0:T(8,128)(2,1)S(1)}, u32[]{:S(2)}, u32[]{:S(2)}) async-start(bf16[4,128,256]{1,2,0:T(8,128)(2,1)} %pad_maximum_fusion.17), calls=%async_computation.2 | async-start | bytes 524288 | tf_op jit(solution)/shard_map/all_to_all | solution.py:399
  492.8 120.7 %all-gather.15.cloned.1.call-start = ((), (), s32[]{:S(2)}) async-start(), calls=%async_computation.17 | async-start | bytes 2359296 | tf_op jit(solution)/shard_map/all_gather | solution.py:403
  605.1 5.4 copy-start.41
  605.1 5.4 copy-start.45
  606.8 30.2 %all-to-all-start.1 = ((bf16[8,128,1024]{2,1,0:T(8,128)(2,1)}), bf16[8,128,1024]{2,1,0:T(8,128)(2,1)S(1)}, u32[]{:S(2)}, u32[]{:S(2)}) async-start(bf16[8,128,1024]{2,1,0:T(8,128)(2,1)} %concatenate.79), calls=%async_computation.3 | async-start | bytes 4194304 | tf_op jit(solution)/shard_map/all_to_all | solution.py:383
  610.4 127.3 %all-reduce.15.cloned.1.call-start = ((), (), s32[]{:S(2)}) async-start(), calls=%async_computation.15 | async-start | bytes 2097152 | tf_op jit(solution)/shard_map/psum | solution.py:340
  712.9 18.5 %copy-start.37 = (f32[128,256]{1,0:T(8,128)S(1)}, f32[128,256]{1,0:T(8,128)}, u32[]{:S(2)}) copy-start(f32[128,256]{1,0:T(8,128)} %param.27) | copy-start | bytes 393220
  712.9 18.6 %copy-start.38 = (f32[128,256]{1,0:T(8,128)S(1)}, f32[128,256]{1,0:T(8,128)}, u32[]{:S(2)}) copy-start(f32[128,256]{1,0:T(8,128)} %param.24) | copy-start | bytes 393220
  713.0 24.8 %copy-start.5 = (bf16[512,1024]{1,0:T(8,128)(2,1)S(1)}, bf16[512,1024]{1,0:T(8,128)(2,1)}, u32[]{:S(2)}) copy-start(bf16[512,1024]{1,0:T(8,128)(2,1)} %param.21) | copy-start | bytes 3145732
  713.0 24.8 %copy-start.52 = (f32[1024]{0:T(1024)S(1)}, f32[1024]{0:T(1024)}, u32[]{:S(2)}) copy-start(f32[1024]{0:T(1024)} %copy-done.50) | copy-start | bytes 12292
  713.0 76.6 %copy-start.49 = (f32[2176]{0:T(1024)S(1)}, f32[2176]{0:T(1024)}, u32[]{:S(2)}) copy-start(f32[2176]{0:T(1024)} %param.38) | copy-start | bytes 26116
  713.0 77.9 %copy-start.7 = (f32[512,1024]{1,0:T(8,128)S(1)}, f32[512,1024]{1,0:T(8,128)}, u32[]{:S(2)}) copy-start(f32[512,1024]{1,0:T(8,128)} %copy-done.6) | copy-start | bytes 6291460
  713.0 85.7 %all-to-all-start.2 = ((bf16[8,128,1024]{2,1,0:T(8,128)(2,1)}), bf16[8,128,1024]{2,1,0:T(8,128)(2,1)}, u32[]{:S(2)}, u32[]{:S(2)}) async-start(bf16[8,128,1024]{2,1,0:T(8,128)(2,1)} %bitcast.37), calls=%async_computation.4 | async-start | bytes 4194304 | tf_op jit(solution)/shard_map/all_to_all | solution.py:411
  790.9 7.1 copy-start.29
  794.0 13.3 %copy-start.27 = (f32[128,1152]{1,0:T(8,128)S(1)}, f32[128,1152]{1,0:T(8,128)}, u32[]{:S(2)}) copy-start(f32[128,1152]{1,0:T(8,128)} %param.29) | copy-start | bytes 1769476
  800.5 13.1 %all-to-all-start.3 = ((bf16[4,128,256]{1,2,0:T(8,128)(2,1)}), bf16[4,128,256]{1,2,0:T(8,128)(2,1)S(1)}, u32[]{:S(2)}, u32[]{:S(2)}) async-start(bf16[4,128,256]{1,2,0:T(8,128)(2,1)} %bitcast.39), calls=%async_computation.5 | async-start | bytes 524288 | tf_op jit(solution)/shard_map/all_to_all | solution.py:414
  804.0 6.4 copy-start.28
  807.3 6.3 copy-start.35
  (33 other events, 96.4 us)
Sparse Core Ops, SparseCore 0:
  10.7 26.1 all-gather.6
  40.5 16.7 all-gather.8
  72.1 51.8 all-reduce.8
  126.5 38.2 all-gather.10
  167.3 29.0 all-gather.12
  207.9 51.7 all-reduce.10
  262.6 51.1 all-reduce.12
  349.6 24.2 reduce-scatter.5
  377.4 65.5 reduce-scatter.7
  446.4 38.4 reduce-scatter.9
  486.9 48.8 all-gather.16
  538.3 27.8 all-gather.14
  613.7 51.1 all-reduce.14
where the time goes:
time: 835 us; the launch traced here: 823 us
  waiting for transfers between devices  381 us (46%)
  matrix products  155 us (19%)
  blocking collectives  121 us (14%)
  other arithmetic  69.3 us (8%)
  local copies, waits for them, and re-layouts  40 us (5%)
  starting transfers between devices  32 us (4%)
  between operations  15.4 us (2%)
  loops' own time  9.64 us (1%)
    psum x1, blocking collectives, body(): gram_rows = lax.psum(gram_rows, 'tensor').astype(HALF_TYPE)  61.1 us
    psum x1, blocking collectives, body(): gain_total = lax.psum(gain_local, ('fsdp', 'context', 'tensor'))  49.6 us
    psum x1, waiting for transfers between devices, body(): lax.psum(attn_part.astype(jnp.bfloat16), 'tensor').astype(jnp.float32)  48.5 us
    psum x1, waiting for transfers between devices, body(): lax.psum(d_second_part.astype(jnp.bfloat16), 'tensor').astype(jnp.float32)  47.7 us
    psum x1, waiting for transfers between devices, body(): ffn_out = lax.psum(ffn_half, 'tensor').astype(jnp.float32)  47.3 us
    reduce_scatter x1, waiting for transfers between devices, body(): lax.psum_scatter(jnp.concatenate([grad_gate_up.astype(jnp.bfloat16), grad...  46.3 us
    all_gather x1, waiting for transfers between devices, body(): lax.all_gather(jnp.concatenate([half_g, half_u], axis=1), plane, axis=0,...  39.1 us
    unnamed x14, waiting for transfers between devices  38 us
  transfers between devices with their start and end apart: 17, of which 12 were waited for; matrix products, arithmetic and copies ran while one was open for 23% of the time, Pallas kernels for 0%

commit v1 on v0

--- a/solution.py
+++ b/solution.py
@@ -119,6 +119,47 @@
                 once.astype(HALF_TYPE), mixer, preferred_element_type=FULL_TYPE
             )
     return (total * inverse).astype(HALF_TYPE)
+
+
+def swap(values, axis, bit):
+    return lax.ppermute(values, axis, [(i, i ^ bit) for i in range(lax.axis_size(axis))])
+
+
+def bits_of(axis):
+    size = lax.axis_size(axis)
+    return [(axis, 1 << power) for power in reversed(range(size.bit_length() - 1))]
+
+
+def plane_gather(shard):
+    along = bits_of("context")
+    context_size = lax.axis_size("context")
+    block = shard[None]
+    offsets = [0]
+    for axis, bit in along[:-1] + bits_of("fsdp") + along[-1:]:
+        other = swap(block, axis, bit)
+        weight = context_size * bit if axis == "fsdp" else bit
+        block = jnp.concatenate([block, other], axis=0)
+        offsets = offsets + [offset ^ weight for offset in offsets]
+    here = lax.axis_index("fsdp") * context_size + lax.axis_index("context")
+    rows = shard.shape[0]
+    whole = jnp.zeros((rows * len(offsets), shard.shape[1]), shard.dtype)
+    for position, offset in enumerate(offsets):
+        start = lax.bitwise_xor(here, offset) * rows
+        whole = lax.dynamic_update_slice_in_dim(whole, block[position], start, axis=0)
+    return whole
+
+
+def swapped_sum(values):
+    for axis in ("context", "fsdp", "tensor"):
+        for name, bit in bits_of(axis):
+            values = values + swap(values, name, bit)
+    return values
+
+
+def scatter_sum(values, axes, pieces):
+    parts = values.reshape(pieces, values.shape[0] // pieces, values.shape[1])
+    arrived = lax.all_to_all(parts, axes, split_axis=0, concat_axis=0, tiled=True)
+    return jnp.sum(arrived.astype(FULL_TYPE), axis=0)
 
 
 def head_rows(values, head_index, group_size):
@@ -181,14 +222,17 @@
     half_d = w_down.astype(HALF_TYPE)
     plane = ("fsdp", "context")
     width_q, width_k, width_f = w_query.shape[1], w_key.shape[1], w_gate.shape[1]
-    full_qkv = lax.all_gather(
-        jnp.concatenate([half_q, half_k, half_v], axis=1), plane, axis=0, tiled=True
-    )
-    full_o = lax.all_gather(half_o, plane, axis=0, tiled=True)
-    full_gu = lax.all_gather(
-        jnp.concatenate([half_g, half_u], axis=1), plane, axis=0, tiled=True
-    )
-    full_d = lax.all_gather(half_d, plane, axis=0, tiled=True)
+    full_qkvo = lax.all_gather(
+        jnp.concatenate([half_q, half_k, half_v, half_o], axis=1), plane, axis=0, tiled=True
+    )
+    full_qkv = full_qkvo[:, : width_q + 2 * width_k]
+    full_o = full_qkvo[:, width_q + 2 * width_k :]
+    wide_half, full_qkv = lax.optimization_barrier(
+        (jnp.concatenate([half_g, half_u, half_d], axis=1), full_qkv)
+    )
+    full_gud = plane_gather(wide_half)
+    full_gu = full_gud[:, : 2 * width_f]
+    full_d = full_gud[:, 2 * width_f :]
     rows = inputs.astype(FULL_TYPE)
     scale_one = rms_scale(rows)
     unit_one = rows * scale_one
@@ -254,21 +298,17 @@
     d_up = (d_hidden * swish).astype(HALF_TYPE)
     d_gate_up = jnp.concatenate([d_gate, d_up], axis=1)
     grad_gate_up = jnp.einsum("td,tf->df", second, d_gate_up, preferred_element_type=FULL_TYPE)
-    wide_grad = lax.psum_scatter(
-        jnp.concatenate(
-            [grad_gate_up.astype(jnp.bfloat16), grad_down.astype(jnp.bfloat16)], axis=1
-        ),
-        plane,
-        scatter_dimension=0,
-        tiled=True,
-    ).astype(jnp.float32)
+    wide_part = jnp.concatenate(
+        [grad_gate_up.astype(jnp.bfloat16), grad_down.astype(jnp.bfloat16)], axis=1
+    )
     d_second_part = jnp.einsum(
         "tf,df->td", d_gate_up, full_gu, preferred_element_type=FULL_TYPE
     )
     d_second = lax.psum(d_second_part.astype(jnp.bfloat16), "tensor").astype(jnp.float32)
-    ffn_half, d_second = lax.optimization_barrier((ffn_part.astype(jnp.bfloat16), d_second))
-    ffn_out = lax.psum(ffn_half, "tensor").astype(jnp.float32)
-    block_out = (resid + ffn_out).astype(HALF_TYPE)
+    wide_part, d_second = lax.optimization_barrier((wide_part, d_second))
+    wide_grad = lax.psum_scatter(
+        wide_part, plane, scatter_dimension=0, tiled=True
+    ).astype(jnp.float32)
     d_resid = cotangent.astype(FULL_TYPE) + norm_back(d_second, unit_two, scale_two, gain_two)
     grad_gain_two = jnp.sum(d_second * unit_two, axis=0)
     d_attn = d_resid.astype(HALF_TYPE)
@@ -302,12 +342,11 @@
         )
     d_key_all = jnp.concatenate(d_key_parts, axis=1)
     d_value_all = jnp.concatenate(d_value_parts, axis=1)
-    key_value_grad = lax.psum_scatter(
+    key_value_grad = scatter_sum(
         jnp.concatenate([d_key_all, d_value_all], axis=1).astype(jnp.bfloat16),
         "context",
-        scatter_dimension=0,
-        tiled=True,
-    ).astype(jnp.float32)
+        context_size,
+    )
     key_grad = key_value_grad[:, :width_k]
     value_grad = key_value_grad[:, width_k:]
     d_value_raw = value_grad.astype(HALF_TYPE)
@@ -327,24 +366,24 @@
     )
     d_qkv = jnp.concatenate([d_query_raw, d_key_raw, d_value_raw], axis=1)
     grad_qkv = jnp.einsum("td,tc->dc", normed, d_qkv, preferred_element_type=FULL_TYPE)
-    narrow_grad = lax.psum_scatter(
+    plane_size = lax.axis_size("fsdp") * context_size
+    narrow_grad = scatter_sum(
         jnp.concatenate([grad_qkv.astype(jnp.bfloat16), grad_out.astype(jnp.bfloat16)], axis=1),
         plane,
-        scatter_dimension=0,
-        tiled=True,
-    ).astype(jnp.float32)
+        plane_size,
+    )
     d_normed_part = jnp.einsum("tc,dc->td", d_qkv, full_qkv, preferred_element_type=FULL_TYPE)
-    d_normed_half, block_out = lax.optimization_barrier(
-        (d_normed_part.astype(jnp.bfloat16), block_out)
-    )
-    d_normed = lax.psum(d_normed_half, "tensor").astype(jnp.float32)
+    d_normed = lax.psum(d_normed_part.astype(jnp.bfloat16), "tensor").astype(jnp.float32)
+    ffn_half, d_normed = lax.optimization_barrier((ffn_part.astype(jnp.bfloat16), d_normed))
+    ffn_out = lax.psum(ffn_half, "tensor").astype(jnp.float32)
+    block_out = (resid + ffn_out).astype(HALF_TYPE)
     input_grad = d_resid + norm_back(d_normed, unit_one, scale_one, gain_one)
     grad_gain_one = jnp.sum(d_normed * unit_one, axis=0)
     first_tensor = (lax.axis_index("tensor") == 0).astype(FULL_TYPE)
     gain_local = jnp.concatenate(
         [grad_gain_one * first_tensor, grad_gain_two * first_tensor, grad_gain_query, grad_gain_key]
     )
-    gain_total = lax.psum(gain_local, ("fsdp", "context", "tensor"))
+    gain_total = swapped_sum(gain_local)
     reduced = (
         narrow_grad[:, :width_q],
         narrow_grad[:, width_q : width_q + width_k],
@@ -358,7 +397,6 @@
         (MU * moment_old + gradient for moment_old, gradient in zip(moments, reduced))
     )
     row_block = w_gate.shape[0]
-    plane_size = lax.axis_size("fsdp") * context_size
     plane_index = lax.axis_index("fsdp") * context_size + lax.axis_index("context")
     wide_all = lax.all_gather(
         jnp.concatenate([moment.astype(HALF_TYPE) for moment in new_moments[4:]], axis=1),
@@ -379,7 +417,16 @@
             for index in range(3)
         ]
     )
-    gram_rows = lax.psum(gram_rows, "tensor").astype(HALF_TYPE)
+    gram_piece = scatter_sum(
+        gram_rows.reshape(3 * row_block, D).astype(HALF_TYPE), "tensor", tensor_size
+    ).astype(HALF_TYPE)
+    gram_rows = lax.all_to_all(
+        jnp.broadcast_to(gram_piece[None], (tensor_size,) + gram_piece.shape),
+        "tensor",
+        split_axis=0,
+        concat_axis=0,
+        tiled=True,
+    ).reshape(3, row_block, D)
     gram = lax.all_to_all(
         jnp.concatenate(
             [gram_rows, jnp.zeros((plane_size - 3, row_block, D), HALF_TYPE)], axis=0
@@ -400,7 +447,7 @@
         .transpose(1, 0, 2)
         .reshape(row_block, tensor_size * width_q)
     )
-    narrow_all = lax.all_gather(narrow_rows, plane, axis=0, tiled=True)
+    narrow_all = plane_gather(narrow_rows)
     ready = lax.cond(
         plane_index < 3,
         lambda gram_arg, narrow_arg: gram_newton_schulz(gram_arg),

time: 835 us -> 722 us (0.86)
  blocking collectives: 121 us -> 0 us
  waiting for transfers between devices: 381 us -> 300 us
  starting transfers between devices: 32 us -> 84.7 us
  local copies, waits for them, and re-layouts: 40 us -> 72.5 us
  other arithmetic: 69.3 us -> 82.8 us
    psum x2 -> x0, blocking collectives: 111 us -> none  [the longest x1 61.1 us: body(): gram_rows = lax.psum(gram_rows, 'tensor').astype(HALF_TYPE)]
    ppermute x0 -> x11, waiting for transfers between devices: none -> 95.2 us  [swap(): lax.ppermute(values, axis, [(i, i ^ bit) for i in range(lax.axis_size(axi...]
    all_gather x4 -> x1, waiting for transfers between devices: 84.2 us -> 23.9 us  [body(): lax.all_gather(jnp.concatenate([half_q, half_k, half_v, half_o], axis=1),...]
    unnamed x14 -> x8, waiting for transfers between devices: 38 us -> 0.13 us
    all_to_all x0 -> x4, waiting for transfers between devices: none -> 35.7 us  [the longest x3 23.9 us: scatter_sum(): lax.all_to_all(parts, axes, split_axis=0, concat_axis=0, tiled=True)]
    psum x1, waiting for transfers between devices: 47.3 us -> 11.6 us  [body(): ffn_out = lax.psum(ffn_half, 'tensor').astype(jnp.float32)]
    all_gather x1, waiting for transfers between devices: 33.2 us -> 0.01 us  [body(): lax.all_gather(jnp.concatenate([moment.astype(HALF_TYPE) for moment in ne...]
    psum x1, waiting for transfers between devices: 48.5 us -> 22.5 us  [body(): lax.psum(attn_part.astype(jnp.bfloat16), 'tensor').astype(jnp.float32)]
  transfers between devices with their start and end apart: 17 -> 27, of which waited for: 12 -> 16; matrix products, arithmetic and copies ran while one was open for 23% -> 35% of each run, Pallas kernels for 0% -> 0%
where the time goes in v1:
time: 722 us; the launch traced here: 716 us
  waiting for transfers between devices  300 us (42%)
  matrix products  152 us (21%)
  starting transfers between devices  84.7 us (12%)
  other arithmetic  82.8 us (11%)
  local copies, waits for them, and re-layouts  72.5 us (10%)
  between operations  15.6 us (2%)
  loops' own time  9.67 us (1%)
    ppermute x11, waiting for transfers between devices, swap(): lax.ppermute(values, axis, [(i, i ^ bit) for i in range(lax.axis_size(axi...  95.2 us
    reduce_scatter x1, waiting for transfers between devices, body(): lax.psum_scatter(wide_part, plane, scatter_dimension=0, tiled=True)  66.5 us
    psum x1, waiting for transfers between devices, body(): lax.psum(d_second_part.astype(jnp.bfloat16), 'tensor').astype(jnp.float32)  37.4 us
    all_to_all x1, starting transfers between devices, body(): lax.all_to_all(ready.reshape(plane_size, row_block, D), plane, split_axis...  35.5 us
    dot_general x4, matrix products, gram_newton_schulz(): jnp.dot(mixer, total.astype(HALF_TYPE), preferred_element_type=FULL_TYPE)  28.7 us
    unnamed x177, local copies, waits for them, and re-layouts  24.8 us
    all_to_all x3, waiting for transfers between devices, scatter_sum(): lax.all_to_all(parts, axes, split_axis=0, concat_axis=0, tiled=True)  23.9 us
    all_gather x1, waiting for transfers between devices, body(): lax.all_gather(jnp.concatenate([half_q, half_k, half_v, half_o], axis=1),...  23.9 us
  transfers between devices with their start and end apart: 27, of which 16 were waited for; matrix products, arithmetic and copies ran while one was open for 35% of the time, Pallas kernels for 0%

profile of v1, /device:TPU:0, one launch (start us, length us, event | category | flops | bytes accessed | tf_op | source)
XLA Modules:
  0.0 716.3 jit_solution(15694179976646766111)
XLA Ops:
  16.2 23.9 %all-gather.4.cloned.1.call-done = bf16[1024,768]{1,0:T(8,128)(2,1)} async-done(((bf16[128,768]{1,0:T(8,128)(2,1)}), bf16[1024,768]{1,0:T(8,128)(2,1)}) %all-gather.4.cloned.1.call-update) | async-done | bytes 1572880 | tf_op jit(solution)/shard_map/all_gather | solution.py:225
  51.2 22.9 %collective-permute-done = bf16[1,128,3456]{2,1,0:T(8,128)(2,1)S(1)} collective-permute-done((bf16[1,128,3456]{2,1,0:T(8,128)(2,1)S(1)}, bf16[1,128,3456]{2,1,0:T(8,128)(2,1)S(1)}, u32[]{:S(2)}, u32[]{:S(2)}) %collective-permute-start) | collective-permute-done | bytes 884768 | tf_op jit(solution)/shard_map/ppermute | solution.py:125
  76.8 4.5 fusion.215
  92.3 2.5 convolution_convert_fusion.5
  95.5 20.3 %collective-permute-done.1 = bf16[2,128,3456]{2,1,0:T(8,128)(2,1)} collective-permute-done((bf16[2,128,3456]{2,1,0:T(8,128)(2,1)}, bf16[2,128,3456]{2,1,0:T(8,128)(2,1)}, u32[]{:S(2)}, u32[]{:S(2)}) %collective-permute-start.1) | collective-permute-done | bytes 1769504 | tf_op jit(solution)/shard_map/ppermute | solution.py:125
  115.8 3.2 pad_maximum_fusion.1
  119.0 3.4 broadcast_in_dim.30
  124.4 22.5 %all-reduce.8.cloned.1.call-done = bf16[512,1024]{1,0:T(8,128)(2,1)} async-done(((bf16[512,1024]{1,0:T(8,128)(2,1)}), bf16[512,1024]{1,0:T(8,128)(2,1)}) %all-reduce.8.cloned.1.call-update) | async-done | bytes 1048592 | tf_op jit(solution)/shard_map/psum | solution.py:281
  161.6 5.2 fusion.102
  166.8 4.8 multiply_convert_fusion.3
  173.0 6.0 fusion.144
  179.0 6.7 convolution_convert_fusion
  187.4 5.7 pad_maximum_fusion
  193.0 37.4 %all-reduce.10.cloned.1.call-done = bf16[512,1024]{1,0:T(8,128)(2,1)} async-done(((bf16[512,1024]{1,0:T(8,128)(2,1)}), bf16[512,1024]{1,0:T(8,128)(2,1)}) %all-reduce.10.cloned.1.call-update) | async-done | bytes 1048592 | tf_op jit(solution)/shard_map/psum | solution.py:307
  232.1 66.5 %reduce-scatter.2.cloned.1.call-done = bf16[128,3456]{1,0:T(8,128)(2,1)} async-done(((bf16[1024,3456]{1,0:T(8,128)(2,1)}), bf16[128,3456]{1,0:T(8,128)(2,1)}) %reduce-scatter.2.cloned.1.call-update) | async-done | bytes 884752 | tf_op jit(solution)/shard_map/reduce_scatter | solution.py:309
  300.0 2.7 fusion.210
  305.7 2.7 multiply_reduce_fusion.2
  313.7 2.7 multiply_reduce_fusion
  316.4 4.3 multiply_convert_fusion
  320.7 6.4 copy.189
  329.0 5.8 multiply_reduce_fusion.1
  336.1 4.1 multiply_convert_fusion.1
  340.3 6.5 copy.188
  347.7 3.3 fusion.120
  357.9 4.7 all-to-all-start
  362.6 3.6 convolution_multiply_fusion.2
  367.1 4.3 convolution_multiply_fusion.3
  386.1 4.2 all-to-all-start.1
  390.3 2.7 fusion.162
  393.0 2.7 fusion.156
  395.7 2.7 fusion.159
  399.3 12.0 %all-to-all-done.1 = bf16[8,128,768]{1,2,0:T(8,128)(2,1)S(1)} async-done(((bf16[8,128,768]{1,2,0:T(8,128)(2,1)}), bf16[8,128,768]{1,2,0:T(8,128)(2,1)S(1)}, u32[]{:S(2)}, u32[]{:S(2)}) %all-to-all-start.1) | async-done | bytes 1572896 | tf_op jit(solution)/shard_map/all_to_all | solution.py:161
  411.3 4.5 all-to-all-start.3
  421.2 11.9 %all-to-all-done.3 = bf16[4,96,1024]{2,1,0:T(8,128)(2,1)S(1)} async-done(((bf16[4,96,1024]{2,1,0:T(8,128)(2,1)}), bf16[4,96,1024]{2,1,0:T(8,128)(2,1)S(1)}, u32[]{:S(2)}, u32[]{:S(2)}) %all-to-all-start.3) | async-done | bytes 786464 | tf_op jit(solution)/shard_map/all_to_all | solution.py:161
  433.2 3.4 all-to-all-start.2
  436.7 6.6 all-to-all-done.2
  444.3 3.5 all-to-all-start.4
  447.8 5.2 collective-permute-start.3
  453.1 11.8 %all-to-all-done.4 = bf16[4,96,1024]{2,1,0:T(8,128)(2,1)S(1)} async-done(((bf16[4,96,1024]{2,1,0:T(8,128)(2,1)}), bf16[4,96,1024]{2,1,0:T(8,128)(2,1)S(1)}, u32[]{:S(2)}, u32[]{:S(2)}) %all-to-all-start.4) | async-done | bytes 786464 | tf_op jit(solution)/shard_map/all_to_all | solution.py:423
  466.4 8.1 %all-to-all-start.5 = ((bf16[8,128,1024]{2,1,0:T(8,128)(2,1)}), bf16[8,128,1024]{2,1,0:T(8,128)(2,1)S(1)}, u32[]{:S(2)}, u32[]{:S(2)}) async-start(bf16[8,128,1024]{2,1,0:T(8,128)(2,1)} %concatenate.104), calls=%async_computation.6 | async-start | bytes 4194304 | tf_op jit(solution)/shard_map/all_to_all | solution.py:430
  476.7 34.8 %collective-permute-done.4 = bf16[2,128,1024]{1,2,0:T(8,128)(2,1)S(1)} collective-permute-done((bf16[2,128,1024]{1,2,0:T(8,128)(2,1)S(1)}, bf16[2,128,1024]{1,2,0:T(8,128)(2,1)S(1)}, u32[]{:S(2)}, u32[]{:S(2)}) %collective-permute-start.4) | collective-permute-done | bytes 524320 | tf_op jit(solution)/shard_map/ppermute | solution.py:125
  512.6 3.0 convolution_convert_fusion.7
  515.7 76.3 %conditional.4 = (bf16[1024,1024]{1,0:T(8,128)(2,1)}) conditional(s32[]{:T(128)} %convert_element_type.467, (bf16[128,4,256]{0,2,1:T(8,128)(2,1)S(1)}, s32[]{:T(128)}, bf16[1,128,1024]{1,2,0:T(8,128)(2,1)S(1)}, s32[]{:T(128)}, bf16[2,128,1024]{1,2,0:T(8,128)(2,1)S(1)}, /*index=5*/s32[]{:T(128)}, s32[]{:T(128)}, bf16[4,128,1024]{1,2,0:T(8,128)(2,1)}, ...), branch_computations={%region_25.27_spmd, %region_27.29_spmd} | conditional | flops 36595302400 | bytes 226500704
  524.3 2.6 fusion.30
  536.0 2.5 add_convert_fusion.12
  540.9 3.2 multiply_add_fusion.6
  544.1 2.5 add_convert_fusion.11
  549.0 2.7 multiply_add_fusion.3
  551.7 2.5 add_convert_fusion.10
  559.0 4.5 fusion.47
  567.9 4.5 fusion.45
  572.3 19.4 %add_multiply_fusion = bf16[1024,1024]{1,0:T(8,128)(2,1)} fusion(f32[]{:T(128)S(6)} %div.46, f32[1024,1024]{1,0:T(8,128)} %fusion.47, f32[1024,1024]{1,0:T(8,128)} %copy-done.71, f32[1024,1024]{1,0:T(8,128)} %fusion.45, f32[1024,1024]{1,0:T(8,128)} %copy-done.72), kind=kOutput, calls=%fused_computation.45 | convolution fusion | flops 4313841664 | bytes 18874372 | tf_op jit(solution)/shard_map/cond/branch_1_fun/dot_general | solution.py:113
  591.9 35.5 %all-to-all-start.6 = ((bf16[8,128,1024]{2,1,0:T(8,128)(2,1)}), bf16[8,128,1024]{2,1,0:T(8,128)(2,1)}, u32[]{:S(2)}, u32[]{:S(2)}) async-start(bf16[8,128,1024]{2,1,0:T(8,128)(2,1)} %bitcast.60), calls=%async_computation.7 | async-start | bytes 4194304 | tf_op jit(solution)/shard_map/all_to_all | solution.py:458
  627.5 4.2 fusion.141
  631.8 2.9 convert_element_type.460
  635.0 3.0 fusion.126
  640.1 13.3 %collective-permute-done.6 = f32[2176]{0:T(1024)S(1)} collective-permute-done((f32[2176]{0:T(1024)S(1)}, f32[2176]{0:T(1024)S(1)}, u32[]{:S(2)}, u32[]{:S(2)}) %collective-permute-start.6) | collective-permute-done | bytes 8736 | tf_op jit(solution)/shard_map/ppermute | solution.py:125
  656.3 2.5 collective-permute-done.8
  675.0 11.6 %all-reduce.14.cloned.1.call-done = bf16[512,1024]{1,0:T(8,128)(2,1)} async-done(((bf16[512,1024]{1,0:T(8,128)(2,1)}), bf16[512,1024]{1,0:T(8,128)(2,1)}) %all-reduce.14.cloned.1.call-update) | async-done | bytes 1048592 | tf_op jit(solution)/shard_map/psum | solution.py:378
  686.7 4.7 fusion.125
  693.2 3.4 all-to-all-start.7
  696.7 3.3 fusion.117
  699.9 3.1 fusion.114
  703.1 3.1 fusion.111
  (357 shorter events, 152.1 us)
Async XLA Ops:
  7.2 7.8 %copy-start.68 = (s32[1,4]{1,0:T(1,128)S(1)}, s32[1,4]{1,0:T(1,128)}, u32[]{:S(2)}) copy-start(s32[1,4]{1,0:T(1,128)} %param.23) | copy-start | bytes 52
  7.2 8.2 %copy-start.3 = (bf16[512,1024]{1,0:T(8,128)(2,1)S(1)}, bf16[512,1024]{1,0:T(8,128)(2,1)}, u32[]{:S(2)}) copy-start(bf16[512,1024]{1,0:T(8,128)(2,1)} %param.21) | copy-start | bytes 3145732
  7.2 8.5 %copy-start.42 = (f32[2176]{0:T(1024)S(1)}, f32[2176]{0:T(1024)}, u32[]{:S(2)}) copy-start(f32[2176]{0:T(1024)} %param.38) | copy-start | bytes 26116
  7.2 32.9 %all-gather.4.cloned.1.call-start = ((), (), s32[]{:S(2)}) async-start(), calls=%async_computation.9 | async-start | bytes 1769472 | tf_op jit(solution)/shard_map/all_gather | solution.py:225
  11.6 65.2 %all-gather.6.cloned.1.call-start = ((), (), s32[]{:S(2)}) async-start(), calls=%async_computation.10 | async-start | bytes 1310720 | tf_op jit(solution)/shard_map/all_gather | solution.py:250
  15.7 26.6 %copy-start.50 = (f32[512]{0:T(512)}, f32[512]{0:T(512)S(1)}, u32[]{:S(2)}) copy-start(f32[512]{0:T(512)S(1)} %add_rsqrt_fusion.3) | copy-start | bytes 6148
  15.8 26.6 %copy-start.64 = (f32[64]{0:T(128)}, f32[64]{0:T(128)S(1)}, u32[]{:S(2)}) copy-start(f32[64]{0:T(128)S(1)} %get-tuple-element.394) | copy-start | bytes 772
  15.8 34.6 %copy-start.62 = (f32[64]{0:T(128)}, f32[64]{0:T(128)S(1)}, u32[]{:S(2)}) copy-start(f32[64]{0:T(128)S(1)} %get-tuple-element.395) | copy-start | bytes 772
  15.8 163.2 %copy-start.45 = (f32[1024]{0:T(1024)}, f32[1024]{0:T(1024)S(1)}, u32[]{:S(2)}) copy-start(f32[1024]{0:T(1024)S(1)} %get-tuple-element.392) | copy-start | bytes 12292
  15.8 368.0 %copy-start.43 = (f32[1024]{0:T(1024)}, f32[1024]{0:T(1024)S(1)}, u32[]{:S(2)}) copy-start(f32[1024]{0:T(1024)S(1)} %get-tuple-element.393) | copy-start | bytes 12292
  44.2 102.7 %all-reduce.8.cloned.1.call-start = ((), (), s32[]{:S(2)}) async-start(), calls=%async_computation.11 | async-start | bytes 2097152 | tf_op jit(solution)/shard_map/psum | solution.py:281
  46.7 27.4 %collective-permute-start = (bf16[1,128,3456]{2,1,0:T(8,128)(2,1)S(1)}, bf16[1,128,3456]{2,1,0:T(8,128)(2,1)S(1)}, u32[]{:S(2)}, u32[]{:S(2)}) collective-permute-start(bf16[1,128,3456]{2,1,0:T(8,128)(2,1)S(1)} %bitcast.268), channel_id=1, source_target_pairs={{0,8},{4,12},{8,0},{12,4},{1,9},{5,13},{9,1},{13,5},{2,10},{6,14},... | collective-permute-start | bytes 2654216 | tf_op jit(solution)/shard_map/ppermute | solution.py:125
  51.2 30.2 %copy-start.29 = (bf16[8,8,2,512]{3,1,2,0:T(8,128)(2,1)}, bf16[8,8,2,512]{3,1,2,0:T(8,128)(2,1)S(1)}, u32[]{:S(2)}) copy-start(bf16[8,8,2,512]{3,1,2,0:T(8,128)(2,1)S(1)} %copy.199) | copy-start | bytes 393220
  51.2 31.4 %copy-start.28 = (bf16[8,8,2,512]{3,1,2,0:T(8,128)(2,1)}, bf16[8,8,2,512]{3,1,2,0:T(8,128)(2,1)S(1)}, u32[]{:S(2)}) copy-start(bf16[8,8,2,512]{3,1,2,0:T(8,128)(2,1)S(1)} %copy.198) | copy-start | bytes 393220
  75.5 40.3 %collective-permute-start.1 = (bf16[2,128,3456]{2,1,0:T(8,128)(2,1)}, bf16[2,128,3456]{2,1,0:T(8,128)(2,1)}, u32[]{:S(2)}, u32[]{:S(2)}) collective-permute-start(bf16[2,128,3456]{2,1,0:T(8,128)(2,1)} %pad_maximum_fusion.3), channel_id=1, source_target_pairs={{0,16},{16,0},{1,17},{17,1},{2,18},{18,2},{3,19},{19,3},{4,20},{20... | collective-permute-start | bytes 5308424 | tf_op jit(solution)/shard_map/ppermute | solution.py:125
  81.3 6.3 copy-start.1
  81.3 6.3 copy-start.53
  94.9 135.5 %all-reduce.10.cloned.1.call-start = ((), (), s32[]{:S(2)}) async-start(), calls=%async_computation.12 | async-start | bytes 2097152 | tf_op jit(solution)/shard_map/psum | solution.py:307
  119.0 33.9 %collective-permute-start.2 = (bf16[4,128,3456]{2,1,0:T(8,128)(2,1)}, bf16[4,128,3456]{2,1,0:T(8,128)(2,1)}, u32[]{:S(2)}, u32[]{:S(2)}) collective-permute-start(bf16[4,128,3456]{2,1,0:T(8,128)(2,1)} %pad_maximum_fusion.1), channel_id=1, source_target_pairs={{0,4},{4,0},{8,12},{12,8},{1,5},{5,1},{9,13},{13,9},{2,6},{6,2},{1... | collective-permute-start | bytes 10616840 | tf_op jit(solution)/shard_map/ppermute | solution.py:125
  148.5 30.5 %copy-start.48 = (f32[512]{0:T(512)}, f32[512]{0:T(512)S(1)}, u32[]{:S(2)}) copy-start(f32[512]{0:T(512)S(1)} %add_rsqrt_fusion.2) | copy-start | bytes 6148
  152.9 8.7 %copy-start.10 = (bf16[512,1024]{1,0:T(8,128)(2,1)S(1)}, bf16[512,1024]{1,0:T(8,128)(2,1)}, u32[]{:S(2)}) copy-start(bf16[512,1024]{1,0:T(8,128)(2,1)} %all-reduce.8.cloned.1.call-done) | copy-start | bytes 3145732
  179.0 119.7 %reduce-scatter.2.cloned.1.call-start = ((), (), s32[]{:S(2)}) async-start(), calls=%async_computation.15 | async-start | bytes 7962624 | tf_op jit(solution)/shard_map/reduce_scatter | solution.py:309
  179.0 6.7 copy-start.22
  179.0 6.7 copy-start.73
  231.8 73.9 %copy-start.9 = (f32[512,1024]{1,0:T(8,128)}, f32[512,1024]{1,0:T(8,128)S(1)}, u32[]{:S(2)}) copy-start(f32[512,1024]{1,0:T(8,128)S(1)} %convert_element_type.449) | copy-start | bytes 6291460
  231.9 158.4 %all-gather.8.cloned.1.call-start = ((), (), s32[]{:S(2)}) async-start(), calls=%async_computation.16 | async-start | bytes 7962624 | tf_op jit(solution)/shard_map/all_gather | solution.py:401
  300.0 5.7 copy-start.46
  305.7 8.0 %slice-start.2 = ((s8[8388608]{0:T(1024)(128)(4,1)}), s8[4194304]{0:T(1024)(128)(4,1)S(1)}, s32[]{:S(2)}) async-start(s8[8388608]{0:T(1024)(128)(4,1)} %bitcast.264), calls=%async_computation.19 | async-start | bytes 8388608
  310.9 67.3 %copy-start.5 = (f32[512,1024]{1,0:T(8,128)}, f32[512,1024]{1,0:T(8,128)S(1)}, u32[]{:S(2)}) copy-start(f32[512,1024]{1,0:T(8,128)S(1)} %multiply_add_fusion.16) | copy-start | bytes 6291460
  320.7 8.2 %copy-start.32 = (bf16[2,8,8,512]{3,2,1,0:T(8,128)(2,1)S(1)}, bf16[2,8,8,512]{3,2,1,0:T(8,128)(2,1)}, u32[]{:S(2)}) copy-start(bf16[2,8,8,512]{3,2,1,0:T(8,128)(2,1)} %get-tuple-element.386) | copy-start | bytes 393220
  328.9 5.9 slice-start
  329.0 7.2 %slice-start.1 = ((s8[8388608]{0:T(1024)(128)(4,1)}), s8[4194304]{0:T(1024)(128)(4,1)S(1)}, s32[]{:S(2)}) async-start(s8[8388608]{0:T(1024)(128)(4,1)} %bitcast.262), calls=%async_computation.18 | async-start | bytes 8388608
  329.0 7.2 %copy-start.47 = (f32[1024]{0:T(1024)S(1)}, f32[1024]{0:T(1024)}, u32[]{:S(2)}) copy-start(f32[1024]{0:T(1024)} %log_add_fusion.1) | copy-start | bytes 12292
  340.3 6.5 copy-start.31
  357.9 21.5 %all-to-all-start = ((bf16[4,512,256]{1,2,0:T(8,128)(2,1)}), bf16[4,512,256]{1,2,0:T(8,128)(2,1)}, u32[]{:S(2)}, u32[]{:S(2)}) async-start(bf16[4,512,256]{1,2,0:T(8,128)(2,1)} %pad_maximum_fusion.8), calls=%async_computation | async-start | bytes 2097152 | tf_op jit(solution)/shard_map/all_to_all | solution.py:161
  371.4 6.7 copy-start.16
  386.1 25.2 %all-to-all-start.1 = ((bf16[8,128,768]{1,2,0:T(8,128)(2,1)}), bf16[8,128,768]{1,2,0:T(8,128)(2,1)S(1)}, u32[]{:S(2)}, u32[]{:S(2)}) async-start(bf16[8,128,768]{1,2,0:T(8,128)(2,1)} %copy_bitcast_fusion), calls=%async_computation.1 | async-start | bytes 3145728 | tf_op jit(solution)/shard_map/all_to_all | solution.py:161
  395.7 20.2 %copy-start.38 = (f32[128,256]{1,0:T(8,128)S(1)}, f32[128,256]{1,0:T(8,128)}, u32[]{:S(2)}) copy-start(f32[128,256]{1,0:T(8,128)} %param.34) | copy-start | bytes 393220
  411.3 21.9 %all-to-all-start.3 = ((bf16[4,96,1024]{2,1,0:T(8,128)(2,1)}), bf16[4,96,1024]{2,1,0:T(8,128)(2,1)S(1)}, u32[]{:S(2)}, u32[]{:S(2)}) async-start(bf16[4,96,1024]{2,1,0:T(8,128)(2,1)} %bitcast.58), calls=%async_computation.4 | async-start | bytes 1572864 | tf_op jit(solution)/shard_map/all_to_all | solution.py:161
  433.2 10.2 %all-to-all-start.2 = ((bf16[4,128,256]{1,2,0:T(8,128)(2,1)}), bf16[4,128,256]{1,2,0:T(8,128)(2,1)S(1)}, u32[]{:S(2)}, u32[]{:S(2)}) async-start(bf16[4,128,256]{1,2,0:T(8,128)(2,1)} %pad_maximum_fusion.20), calls=%async_computation.3 | async-start | bytes 524288 | tf_op jit(solution)/shard_map/all_to_all | solution.py:446
  444.3 20.5 %all-to-all-start.4 = ((bf16[4,96,1024]{2,1,0:T(8,128)(2,1)}), bf16[4,96,1024]{2,1,0:T(8,128)(2,1)S(1)}, u32[]{:S(2)}, u32[]{:S(2)}) async-start(bf16[4,96,1024]{2,1,0:T(8,128)(2,1)} %broadcast_in_dim.32), calls=%async_computation.5 | async-start | bytes 1572864 | tf_op jit(solution)/shard_map/all_to_all | solution.py:423
  447.8 26.8 %collective-permute-start.3 = (bf16[1,128,1024]{1,2,0:T(8,128)(2,1)S(1)}, bf16[1,128,1024]{1,2,0:T(8,128)(2,1)S(1)}, u32[]{:S(2)}, u32[]{:S(2)}) collective-permute-start(bf16[1,128,1024]{1,2,0:T(8,128)(2,1)S(1)} %bitcast.273), channel_id=1, source_target_pairs={{0,8},{4,12},{8,0},{12,4},{1,9},{5,13},{9,1},{13,5},{2,10},{6,14},... | collective-permute-start | bytes 786440 | tf_op jit(solution)/shard_map/ppermute | solution.py:125
  466.4 46.2 %copy-start.40 = (bf16[512,128]{0,1:T(8,128)(2,1)S(1)}, bf16[512,128]{0,1:T(8,128)(2,1)}, u32[]{:S(2)}) copy-start(bf16[512,128]{0,1:T(8,128)(2,1)} %copy-done.39) | copy-start | bytes 393220
  466.4 49.2 %all-to-all-start.5 = ((bf16[8,128,1024]{2,1,0:T(8,128)(2,1)}), bf16[8,128,1024]{2,1,0:T(8,128)(2,1)S(1)}, u32[]{:S(2)}, u32[]{:S(2)}) async-start(bf16[8,128,1024]{2,1,0:T(8,128)(2,1)} %concatenate.104), calls=%async_computation.6 | async-start | bytes 4194304 | tf_op jit(solution)/shard_map/all_to_all | solution.py:430
  474.5 157.3 %all-reduce.12.cloned.1.call-start = ((), (), s32[]{:S(2)}) async-start(), calls=%async_computation.13 | async-start | bytes 2097152 | tf_op jit(solution)/shard_map/psum | solution.py:376
  474.6 36.8 %collective-permute-start.4 = (bf16[2,128,1024]{1,2,0:T(8,128)(2,1)S(1)}, bf16[2,128,1024]{1,2,0:T(8,128)(2,1)S(1)}, u32[]{:S(2)}, u32[]{:S(2)}) collective-permute-start(bf16[2,128,1024]{1,2,0:T(8,128)(2,1)S(1)} %pad_maximum_fusion.15), channel_id=1, source_target_pairs={{0,16},{16,0},{1,17},{17,1},{2,18},{18,2},{3,19},{19,3},{4,20},{20... | collective-permute-start | bytes 1572872 | tf_op jit(solution)/shard_map/ppermute | solution.py:125
  512.6 3.1 collective-permute-start.5
  591.9 35.6 %copy-start.74 = (bf16[512,1152]{1,0:T(8,128)(2,1)S(1)}, bf16[512,1152]{1,0:T(8,128)(2,1)}, u32[]{:S(2)}) copy-start(bf16[512,1152]{1,0:T(8,128)(2,1)} %get-tuple-element.355) | copy-start | bytes 3538948
  591.9 99.4 %all-to-all-start.6 = ((bf16[8,128,1024]{2,1,0:T(8,128)(2,1)}), bf16[8,128,1024]{2,1,0:T(8,128)(2,1)}, u32[]{:S(2)}, u32[]{:S(2)}) async-start(bf16[8,128,1024]{2,1,0:T(8,128)(2,1)} %bitcast.60), calls=%async_computation.7 | async-start | bytes 4194304 | tf_op jit(solution)/shard_map/all_to_all | solution.py:458
  627.5 59.2 %all-reduce.14.cloned.1.call-start = ((), (), s32[]{:S(2)}) async-start(), calls=%async_computation.14 | async-start | bytes 2097152 | tf_op jit(solution)/shard_map/psum | solution.py:378
  631.8 38.6 %copy-start.27 = (f32[128,256]{0,1:T(8,128)S(1)}, f32[128,256]{0,1:T(8,128)}, u32[]{:S(2)}) copy-start(f32[128,256]{0,1:T(8,128)} %get-tuple-element.373) | copy-start | bytes 393220
  634.7 39.5 %copy-start.26 = (f32[128,256]{0,1:T(8,128)S(1)}, f32[128,256]{0,1:T(8,128)}, u32[]{:S(2)}) copy-start(f32[128,256]{0,1:T(8,128)} %get-tuple-element.339) | copy-start | bytes 393220
  634.7 51.9 %copy-start.6 = (f32[512,1024]{1,0:T(8,128)S(1)}, f32[512,1024]{1,0:T(8,128)}, u32[]{:S(2)}) copy-start(f32[512,1024]{1,0:T(8,128)} %copy-done.5) | copy-start | bytes 6291460
  638.1 15.3 %collective-permute-start.6 = (f32[2176]{0:T(1024)S(1)}, f32[2176]{0:T(1024)S(1)}, u32[]{:S(2)}, u32[]{:S(2)}) collective-permute-start(f32[2176]{0:T(1024)S(1)} %concatenate.105), channel_id=1, source_target_pairs={{0,8},{4,12},{8,0},{12,4},{1,9},{5,13},{9,1},{13,5},{2,10},{6,14},... | collective-permute-start | bytes 26120 | tf_op jit(solution)/shard_map/ppermute | solution.py:125
  653.4 1.7 collective-permute-start.7
  655.1 3.7 collective-permute-start.8
  658.8 5.8 collective-permute-start.9
  665.3 3.8 collective-permute-start.10
  691.4 8.6 %copy-start.24 = (f32[128,1152]{1,0:T(8,128)S(1)}, f32[128,1152]{1,0:T(8,128)}, u32[]{:S(2)}) copy-start(f32[128,1152]{1,0:T(8,128)} %param.29) | copy-start | bytes 1769476
  693.2 13.0 %all-to-all-start.7 = ((bf16[4,128,256]{1,2,0:T(8,128)(2,1)}), bf16[4,128,256]{1,2,0:T(8,128)(2,1)S(1)}, u32[]{:S(2)}, u32[]{:S(2)}) async-start(bf16[4,128,256]{1,2,0:T(8,128)(2,1)} %bitcast.62), calls=%async_computation.8 | async-start | bytes 524288 | tf_op jit(solution)/shard_map/all_to_all | solution.py:461
  696.7 6.4 copy-start.25
  699.9 6.3 copy-start.30
  699.9 7.1 copy-start.35
  699.9 7.1 copy-start.36
  (44 other events, 144.2 us)
Sparse Core Ops, SparseCore 0:
  11.7 28.3 all-gather.3
  44.3 22.4 all-gather.5
  95.0 51.8 all-reduce.7
  179.1 51.2 all-reduce.9
  233.7 64.8 reduce-scatter.1
  303.9 48.8 all-gather.7
  515.8 50.0 all-reduce.11
  634.9 51.7 all-reduce.13
